TPU v7x, 256 devices: a whole 4x4x8 slice. The times are simulated.
256 devices in a mesh: row: 16 (over z, x_hi), col: 16 (over x_lo, y, core).
Axes of the slice: x: 4 (x_hi: 2, x_lo: 2; x = x_hi * 2 + x_lo), y: 4, z: 8, core: 2. Of those that a mesh axis runs over, the one named last changes fastest.
Arguments:
- acquired_tiles: bfloat16 [4, 262144, 1024], P(None, ('row', 'col')), may hold values from -24 to 24
- row_live: int32 [4, 262144], P(None, ('row', 'col')), may hold values from 0 to 1, as said below
- col_live: int32 [4, 262144], P(None, ('row', 'col')), may hold values 0 or 1
- row_order: int32 [16], replicated, may hold values from 0 to 15, as said below
- source_init: float32 [262144, 256], P(('row', 'col')), may hold values from -3 to 3
- receiver_init: float32 [262144, 256], P(('row', 'col')), may hold values from -3 to 3
Outputs:
- sources: float32 [262144, 256], P(('row', 'col'))
- receivers: float32 [262144, 256], P(('row', 'col'))
Inputs may be any that keep to these rules, and one draw needn't show every extreme that they name: `row_live`: 1 where the source of that row is recorded in that stratum's tile; sources go missing singly and in whole aligned lines of 128 rows, and the share of missing lines differs from block to block. `row_order`: each number once.
All inputs are finite; a program needn't handle non-finite values. No bound on the sum of `col_live` on one device may be relied on, other than what follows from the above.
Results may differ from a plain program's by a relative error of at most 0.00096.
Values sent between devices are 32-bit elements; how exact they have to be, the bound alone decides.
No kernel may reach another device: no remote copies, remote signals or barrier semaphores. Data moves between devices by JAX's collectives and lax.ppermute only.
A program may use at most 128 MiB of HBM per device.

v0:
```python
import jax
import jax.numpy as jnp
from jax import lax
from jax.sharding import PartitionSpec as P

STEPS = 2


def from_behind(block, axis, distance):
    devices = range(lax.axis_size(axis))
    route = [((i - distance) % len(devices), i) for i in devices]
    return lax.ppermute(block, axis, route)


def fit_dense(src_block, rec_block, acquired, live_rows, live_cols):
    weights = live_rows.astype(jnp.float32)[:, None] * live_cols.astype(jnp.float32)[None, :]
    observed = acquired.astype(jnp.float32)
    step_size = 1.0 / (acquired.shape[1] + 2 * src_block.shape[1])
    for iteration in range(STEPS):
        src_half = src_block.astype(jnp.bfloat16)
        rec_half = rec_block.astype(jnp.bfloat16)
        predicted = lax.dot_general(
            src_half, rec_half, (((1,), (1,)), ((), ())), preferred_element_type=jnp.float32
        )
        misfit = (weights * (observed - predicted)).astype(jnp.bfloat16)
        grad_src = jnp.dot(misfit, rec_half, preferred_element_type=jnp.float32)
        grad_rec = lax.dot_general(
            misfit, src_half, (((0,), (0,)), ((), ())), preferred_element_type=jnp.float32
        )
        src_block = src_block + step_size * grad_src
        rec_block = rec_block + step_size * grad_rec
    return (src_block, rec_block)


def reassign(rec_block, row_order):
    block_rows, rank_width = rec_block.shape
    pieces = lax.all_to_all(
        rec_block.reshape(1, block_rows, rank_width), "row", split_axis=1, concat_axis=0, tiled=True
    )
    pieces = jnp.take(pieces, row_order, axis=0)
    returned = lax.all_to_all(pieces, "row", split_axis=0, concat_axis=1, tiled=True)
    return returned.reshape(block_rows, rank_width)


def local(acquired_tiles, row_live, col_live, row_order, source_init, receiver_init):
    src_block = source_init
    rec_block = receiver_init
    strata = acquired_tiles.shape[0]
    for stratum in range(strata):
        src_block, rec_block = fit_dense(
            src_block, rec_block, acquired_tiles[stratum], row_live[stratum], col_live[stratum]
        )
        if stratum + 1 < strata:
            rec_block = from_behind(rec_block, ("row", "col"), 1)
            if stratum == 1:
                rec_block = reassign(rec_block, row_order)
    return (src_block, rec_block)


def solution(mesh):
    placed = (
        P(None, ("row", "col"), None),
        P(None, ("row", "col")),
        P(None, ("row", "col")),
        P(),
        P(("row", "col"), None),
        P(("row", "col"), None),
    )
    return jax.shard_map(
        local,
        mesh=mesh,
        in_specs=placed,
        out_specs=(P(("row", "col"), None), P(("row", "col"), None)),
        check_vma=False,
    )
```

profile of v0, /device:TPU:0, one launch (start us, length us, event | category | flops | bytes accessed | tf_op | source)
XLA Modules:
  0.0 158.2 jit_solution(6122432359000715010)
XLA Ops:
  0.6 0.9 slice_convert_fusion.1
  1.5 0.9 slice_convert_fusion
  2.4 3.2 %fusion = bf16[1024,1024]{1,0:T(8,128)(2,1)S(1)} fusion(f32[1024]{0:T(1024)S(1)} %bitcast.62, f32[1024]{0:T(1024)S(1)} %bitcast.60, bf16[4,1024,1024]{2,1,0:T(8,128)(2,1)} %param.6, f32[1024,256]{1,0:T(8,128)} %param.11, f32[1024,256]{1,0:T(8,128)} %param.10), kind=kOutput, calls=%fused_computation.17 | convolution fusion | flops 542638080 | bytes 6299648 | tf_op jit(solution)/shard_map/dot_general | solution.py:22
  5.7 0.7 fusion.22
  7.9 1.5 slice-done.1
  9.4 0.9 fusion.1
  10.3 0.7 fusion.20
  11.9 20.0 %collective-permute-done = f32[1024,256]{1,0:T(8,128)S(1)} collective-permute-done((f32[1024,256]{1,0:T(8,128)S(1)}, f32[1024,256]{1,0:T(8,128)S(1)}, u32[]{:S(2)}, u32[]{:S(2)}) %collective-permute-start) | collective-permute-done | bytes 1048608 | tf_op jit(solution)/shard_map/ppermute | solution.py:12
  31.8 0.9 fusion.2
  32.7 0.7 fusion.18
  34.2 0.9 fusion.3
  35.2 0.8 fusion.16
  36.0 19.6 %collective-permute-done.1 = f32[1024,256]{1,0:T(8,128)S(1)} collective-permute-done((f32[1024,256]{1,0:T(8,128)S(1)}, f32[1024,256]{1,0:T(8,128)S(1)}, u32[]{:S(2)}, u32[]{:S(2)}) %collective-permute-start.1) | collective-permute-done | bytes 1048608 | tf_op jit(solution)/shard_map/ppermute | solution.py:12
  55.7 2.0 %copy.8 = f32[1,1024,256]{2,0,1:T(1,128)} copy(f32[1,1024,256]{2,1,0:T(8,128)S(1)} %bitcast.47) | data formatting | bytes 2097152 | tf_op jit(solution)/shard_map/reshape | solution.py:38
  57.7 5.9 %all-to-all-start = ((f32[1,1024,256]{2,0,1:T(1,128)}), f32[1,1024,256]{2,0,1:T(1,128)}, u32[]{:S(2)}, u32[]{:S(2)}) async-start(f32[1,1024,256]{2,0,1:T(1,128)} %copy.8), calls=%async_computation | async-start | bytes 2097152 | tf_op jit(solution)/shard_map/all_to_all | solution.py:37
  63.6 20.4 %all-to-all-done = f32[1,1024,256]{2,0,1:T(1,128)} async-done(((f32[1,1024,256]{2,0,1:T(1,128)}), f32[1,1024,256]{2,0,1:T(1,128)}, u32[]{:S(2)}, u32[]{:S(2)}) %all-to-all-start) | async-done | bytes 1048608 | tf_op jit(solution)/shard_map/all_to_all | solution.py:37
  84.0 2.3 %copy.9 = f32[1,1024,256]{2,1,0:T(8,128)} copy(f32[1,1024,256]{2,0,1:T(1,128)} %all-to-all-done) | data formatting | bytes 2097152
  86.3 2.8 %gather_fusion = f32[16,64,256]{2,1,0:T(8,128)} fusion(f32[16,64,256]{2,1,0:T(8,128)} %bitcast.46, s32[1024]{0:T(1024)S(1)} %pad_clamp_fusion), kind=kCustom, calls=%fused_computation | custom fusion | bytes 2097216 | tf_op jit(solution)/shard_map/jit(_take)/gather | solution.py:40
  89.1 2.3 %broadcast_select_fusion = f32[16,64,256]{2,1,0:T(8,128)} fusion(f32[16,64,256]{2,1,0:T(8,128)} %gather_fusion, pred[16]{0:T(512)(128)(4,1)S(1)} %compare_and_fusion), kind=kLoop, calls=%fused_computation.58 | loop fusion | flops 262144 | bytes 2097168 | tf_op jit(solution)/shard_map/jit(_take)/select_n | solution.py:40
  91.4 4.5 %all-to-all-start.1 = ((f32[16,64,256]{2,1,0:T(8,128)}), f32[16,64,256]{2,1,0:T(8,128)}, u32[]{:S(2)}, u32[]{:S(2)}) async-start(f32[16,64,256]{2,1,0:T(8,128)} %broadcast_select_fusion), calls=%async_computation.1 | async-start | bytes 2097152 | tf_op jit(solution)/shard_map/all_to_all | solution.py:41
  95.9 2.9 %fusion.17 = f32[1024,256]{1,0:T(8,128)} fusion(f32[1024,256]{1,0:T(8,128)S(1)} %fusion.19, bf16[1024,1024]{1,0:T(8,128)(2,1)S(1)} %fusion.3, f32[1024,256]{1,0:T(8,128)} %copy-done.1), kind=kOutput, calls=%fused_computation.44 | convolution fusion | flops 537657344 | bytes 5242880 | tf_op jit(solution)/shard_map/dot_general | solution.py:26
  98.8 18.1 %all-to-all-done.1 = f32[16,64,256]{2,1,0:T(8,128)} async-done(((f32[16,64,256]{2,1,0:T(8,128)}), f32[16,64,256]{2,1,0:T(8,128)}, u32[]{:S(2)}, u32[]{:S(2)}) %all-to-all-start.1) | async-done | bytes 1048608 | tf_op jit(solution)/shard_map/all_to_all | solution.py:41
  116.9 1.3 bitcast_convert_fusion
  118.2 2.9 %fusion.4 = bf16[1024,1024]{1,0:T(8,128)(2,1)S(1)} fusion(bf16[1024,256]{1,0:T(8,128)(2,1)S(1)} %bitcast_convert_fusion, f32[1024]{0:T(1024)S(1)} %bitcast.54, f32[1024]{0:T(1024)S(1)} %bitcast.52, bf16[4,1024,1024]{2,1,0:T(8,128)(2,1)} %param.6, f32[1024,256]{1,0:T(8,128)} %fusion.17), kind=kOutput, calls=%fused_computation.21 | convolution fusion | flops 542375936 | bytes 5775360 | tf_op jit(solution)/shard_map/dot_general | solution.py:22
  121.9 2.3 %fusion.14 = f32[1024,256]{1,0:T(8,128)S(1)} fusion(f32[1024,256]{1,0:T(8,128)} %bitcast.12, bf16[1024,1024]{1,0:T(8,128)(2,1)S(1)} %fusion.4, f32[1024,256]{1,0:T(8,128)S(1)} %copy-done), kind=kOutput, calls=%fused_computation.38 | convolution fusion | flops 537657344 | bytes 5242880 | tf_op jit(solution)/shard_map/dot_general | solution.py:27
  124.3 0.9 fusion.5
  125.2 0.7 fusion.12
  126.8 24.7 %collective-permute-done.2 = f32[1024,256]{1,0:T(8,128)S(1)} collective-permute-done((f32[1024,256]{1,0:T(8,128)S(1)}, f32[1024,256]{1,0:T(8,128)S(1)}, u32[]{:S(2)}, u32[]{:S(2)}) %collective-permute-start.2) | collective-permute-done | bytes 1048608 | tf_op jit(solution)/shard_map/ppermute | solution.py:12
  151.5 0.9 fusion.6
  153.9 0.9 fusion.7
  154.8 1.7 %fusion.8 = f32[1024,256]{1,0:T(8,128)} fusion(f32[1024,256]{1,0:T(8,128)S(1)} %fusion.10, bf16[1024,1024]{1,0:T(8,128)(2,1)S(1)} %fusion.7, f32[1024,256]{1,0:T(8,128)S(1)} %fusion.11), kind=kOutput, calls=%fused_computation.26 | convolution fusion | flops 537657344 | bytes 5242880 | tf_op jit(solution)/shard_map/dot_general | solution.py:27
  156.5 1.7 %fusion.9 = f32[1024,256]{1,0:T(8,128)} fusion(f32[1024,256]{1,0:T(8,128)S(1)} %fusion.11, bf16[1024,1024]{1,0:T(8,128)(2,1)S(1)} %fusion.7, f32[1024,256]{1,0:T(8,128)S(1)} %fusion.10), kind=kOutput, calls=%fused_computation.28 | convolution fusion | flops 537657344 | bytes 5242880 | tf_op jit(solution)/shard_map/dot_general | solution.py:26
  (32 shorter events, 6.0 us)
Async XLA Ops:
  2.4 3.3 %copy-start.2 = (f32[1024,256]{1,0:T(8,128)S(1)}, f32[1024,256]{1,0:T(8,128)}, u32[]{:S(2)}) copy-start(f32[1024,256]{1,0:T(8,128)} %param.10) | copy-start | bytes 3145732
  2.4 3.3 %copy-start.3 = (f32[1024,256]{1,0:T(8,128)S(1)}, f32[1024,256]{1,0:T(8,128)}, u32[]{:S(2)}) copy-start(f32[1024,256]{1,0:T(8,128)} %param.11) | copy-start | bytes 3145732
  5.7 2.2 %slice-start = ((s8[8388608]{0:T(1024)(128)(4,1)}), s8[4194304]{0:T(1024)(128)(4,1)S(1)}, s32[]{:S(2)}) async-start(s8[8388608]{0:T(1024)(128)(4,1)} %bitcast.64), calls=%async_computation.2 | async-start | bytes 8388608
  6.5 2.9 %slice-start.1 = ((s8[8388608]{0:T(1024)(128)(4,1)}), s8[4194304]{0:T(1024)(128)(4,1)S(1)}, s32[]{:S(2)}) async-start(s8[8388608]{0:T(1024)(128)(4,1)} %bitcast.64), calls=%async_computation.3 | async-start | bytes 8388608
  11.0 20.8 %collective-permute-start = (f32[1024,256]{1,0:T(8,128)S(1)}, f32[1024,256]{1,0:T(8,128)S(1)}, u32[]{:S(2)}, u32[]{:S(2)}) collective-permute-start(f32[1024,256]{1,0:T(8,128)S(1)} %fusion.20), channel_id=1, source_target_pairs={{255,0},{0,1},{1,2},{2,3},{3,4},{4,5},{5,6},{6,7},{7,8},{8,9},{9,1... | collective-permute-start | bytes 3145736 | tf_op jit(solution)/shard_map/ppermute | solution.py:12
  33.5 1.7 %copy-start.1 = (f32[1024,256]{1,0:T(8,128)}, f32[1024,256]{1,0:T(8,128)S(1)}, u32[]{:S(2)}) copy-start(f32[1024,256]{1,0:T(8,128)S(1)} %fusion.18) | copy-start | bytes 3145732
  35.9 19.7 %collective-permute-start.1 = (f32[1024,256]{1,0:T(8,128)S(1)}, f32[1024,256]{1,0:T(8,128)S(1)}, u32[]{:S(2)}, u32[]{:S(2)}) collective-permute-start(f32[1024,256]{1,0:T(8,128)S(1)} %fusion.16), channel_id=1, source_target_pairs={{255,0},{0,1},{1,2},{2,3},{3,4},{4,5},{5,6},{6,7},{7,8},{8,9},{9,1... | collective-permute-start | bytes 3145736 | tf_op jit(solution)/shard_map/ppermute | solution.py:12
  55.7 7.9 %copy-start.4 = (s32[16]{0:T(128)S(1)}, s32[16]{0:T(128)}, u32[]{:S(2)}) copy-start(s32[16]{0:T(128)} %param.9) | copy-start | bytes 196
  57.7 26.3 %all-to-all-start = ((f32[1,1024,256]{2,0,1:T(1,128)}), f32[1,1024,256]{2,0,1:T(1,128)}, u32[]{:S(2)}, u32[]{:S(2)}) async-start(f32[1,1024,256]{2,0,1:T(1,128)} %copy.8), calls=%async_computation | async-start | bytes 2097152 | tf_op jit(solution)/shard_map/all_to_all | solution.py:37
  91.4 25.5 %all-to-all-start.1 = ((f32[16,64,256]{2,1,0:T(8,128)}), f32[16,64,256]{2,1,0:T(8,128)}, u32[]{:S(2)}, u32[]{:S(2)}) async-start(f32[16,64,256]{2,1,0:T(8,128)} %broadcast_select_fusion), calls=%async_computation.1 | async-start | bytes 2097152 | tf_op jit(solution)/shard_map/all_to_all | solution.py:41
  118.2 3.0 %copy-start = (f32[1024,256]{1,0:T(8,128)S(1)}, f32[1024,256]{1,0:T(8,128)}, u32[]{:S(2)}) copy-start(f32[1024,256]{1,0:T(8,128)} %fusion.17) | copy-start | bytes 3145732
  118.2 6.0 %slice-start.2 = ((s8[8388608]{0:T(1024)(128)(4,1)}), s8[4194304]{0:T(1024)(128)(4,1)S(1)}, s32[]{:S(2)}) async-start(s8[8388608]{0:T(1024)(128)(4,1)} %bitcast.66), calls=%async_computation.4 | async-start | bytes 8388608
  121.2 3.0 %slice-start.3 = ((s8[8388608]{0:T(1024)(128)(4,1)}), s8[4194304]{0:T(1024)(128)(4,1)S(1)}, s32[]{:S(2)}) async-start(s8[8388608]{0:T(1024)(128)(4,1)} %bitcast.66), calls=%async_computation.5 | async-start | bytes 8388608
  126.0 25.5 %collective-permute-start.2 = (f32[1024,256]{1,0:T(8,128)S(1)}, f32[1024,256]{1,0:T(8,128)S(1)}, u32[]{:S(2)}, u32[]{:S(2)}) collective-permute-start(f32[1024,256]{1,0:T(8,128)S(1)} %fusion.12), channel_id=1, source_target_pairs={{255,0},{0,1},{1,2},{2,3},{3,4},{4,5},{5,6},{6,7},{7,8},{8,9},{9,1... | collective-permute-start | bytes 3145736 | tf_op jit(solution)/shard_map/ppermute | solution.py:12
where the time goes:
time: 161 us; the launch traced here: 158 us
  waiting for transfers between devices  103 us (64%)
  matrix products  29.1 us (18%)
  starting transfers between devices  10.6 us (7%)
  local copies, waits for them, and re-layouts  9.34 us (6%)
  other arithmetic  5.4 us (3%)
    ppermute x3, waiting for transfers between devices, from_behind(): return lax.ppermute(block, axis, route)  64.3 us
    all_to_all x1, waiting for transfers between devices, reassign(): lax.all_to_all(rec_block.reshape(1, block_rows, rank_width), 'row', split...  20.4 us
    all_to_all x1, waiting for transfers between devices, reassign(): lax.all_to_all(pieces, 'row', split_axis=0, concat_axis=1, tiled=True)  18.1 us
    dot_general x8, matrix products, fit_dense(): lax.dot_general(src_half, rec_half, (((1,), (1,)), ((), ())), preferred_e...  11.8 us
    dot_general x8, matrix products, fit_dense(): grad_src = jnp.dot(misfit, rec_half, preferred_element_type=jnp.float32)  8.88 us
    dot_general x8, matrix products, fit_dense(): lax.dot_general(misfit, src_half, (((0,), (0,)), ((), ())), preferred_ele...  8.48 us
    all_to_all x1, starting transfers between devices, reassign(): lax.all_to_all(rec_block.reshape(1, block_rows, rank_width), 'row', split...  5.86 us
    all_to_all x1, starting transfers between devices, reassign(): lax.all_to_all(pieces, 'row', split_axis=0, concat_axis=1, tiled=True)  4.52 us
  transfers between devices with their start and end apart: 5, of which 5 were waited for; matrix products, arithmetic and copies ran while one was open for 3% of the time, Pallas kernels for 0%

commit v1 on v0

v1 whole, which is shorter than its diff:
```python
import functools

import jax
import jax.numpy as jnp
from jax import lax
from jax.experimental import pallas as pl
from jax.experimental.pallas import tpu as pltpu
from jax.sharding import PartitionSpec as P

STEPS = 2
CHUNKS = 2
MIB = 1024 * 1024


def column_of(mask_row, width):
    tall = jnp.broadcast_to(mask_row.astype(jnp.float32), (8, mask_row.shape[1])).T
    return jnp.broadcast_to(tall[:, 0:1], (mask_row.shape[1], width))


def step_body(stratum, part, width, parts, joined, step_size, *refs):
    src_ref, tile_ref, rows_ref, cols_ref = refs[:4]
    rec_refs = refs[4 : 4 + joined]
    grad_ref = refs[4 + joined] if part else None
    sum_ref, new_rec_ref = refs[-2:]
    rank = src_ref.shape[1]
    window = slice(part * width, (part + 1) * width)
    live_rows = column_of(rows_ref[stratum : stratum + 1, :], rank)
    live_cols = column_of(cols_ref[stratum : stratum + 1, window], rank)
    src = src_ref[...]
    if joined > 1:
        rec = jnp.concatenate([ref[...] for ref in rec_refs], 0)
    elif rec_refs[0].shape[0] == width:
        rec = rec_refs[0][...]
    else:
        rec = rec_refs[0][window, :]
    src_half = src.astype(jnp.bfloat16)
    rec_half = rec.astype(jnp.bfloat16)
    src_live = (src * live_rows).astype(jnp.bfloat16)
    rec_live = (rec * live_cols).astype(jnp.bfloat16)
    predicted = lax.dot_general(
        src_half, rec_half, (((1,), (1,)), ((), ())), preferred_element_type=jnp.float32
    )
    misfit = (tile_ref[:, window].astype(jnp.float32) - predicted).astype(jnp.bfloat16)
    grad_src = jnp.dot(misfit, rec_live, preferred_element_type=jnp.float32)
    grad_rec = lax.dot_general(
        misfit, src_live, (((0,), (0,)), ((), ())), preferred_element_type=jnp.float32
    )
    new_rec_ref[...] = rec + (step_size * live_cols) * grad_rec
    if grad_ref is not None:
        grad_src = grad_src + grad_ref[...]
    if part == parts - 1:
        sum_ref[...] = src + (step_size * live_rows) * grad_src
    else:
        sum_ref[...] = grad_src


def step_part(stratum, part, parts, src, recs, tile, rows, cols, grad):
    size, rank = src.shape
    width = tile.shape[1] // parts
    step_size = 1.0 / (tile.shape[1] + 2 * rank)
    operands = [src, tile, rows, cols, *recs] + ([grad] if part else [])
    whole = pl.BlockSpec(memory_space=pltpu.VMEM)
    return pl.pallas_call(
        functools.partial(
            step_body, stratum, part, width, parts, len(recs), step_size
        ),
        out_shape=(
            jax.ShapeDtypeStruct((size, rank), jnp.float32),
            jax.ShapeDtypeStruct((width, rank), jnp.float32),
        ),
        in_specs=[whole] * len(operands),
        out_specs=(whole, whole),
        compiler_params=pltpu.CompilerParams(vmem_limit_bytes=28 * MIB),
        cost_estimate=pl.CostEstimate(
            flops=6 * size * width * rank,
            bytes_accessed=2 * size * width + 12 * size * rank,
            transcendentals=0,
        ),
    )(*operands)


def step(stratum, parts, src, recs, tile, rows, cols):
    grad, news = None, []
    for part in range(parts):
        mine = [recs[part]] if len(recs) == parts else recs
        grad, new = step_part(stratum, part, parts, src, mine, tile, rows, cols, grad)
        news.append(new)
    return grad, news


def pick_body(index_ref, pieces_ref, out_ref, sems):
    copies = [
        pltpu.make_async_copy(pieces_ref.at[index_ref[j]], out_ref.at[j], sems.at[j])
        for j in range(out_ref.shape[0])
    ]
    for copy in copies:
        copy.start()
    for copy in copies:
        copy.wait()


def pick(pieces, index):
    return pl.pallas_call(
        pick_body,
        out_shape=jax.ShapeDtypeStruct(pieces.shape, pieces.dtype),
        in_specs=[
            pl.BlockSpec(memory_space=pltpu.SMEM),
            pl.BlockSpec(memory_space=pl.ANY),
        ],
        out_specs=pl.BlockSpec(memory_space=pl.ANY),
        scratch_shapes=[pltpu.SemaphoreType.DMA((pieces.shape[0],))],
        cost_estimate=pl.CostEstimate(
            flops=0, bytes_accessed=2 * 4 * pieces.size, transcendentals=0
        ),
    )(index, pieces)


def onward(block, axes):
    count = lax.axis_size(axes)
    return lax.ppermute(block, axes, [(i, (i + 1) % count) for i in range(count)])


def reassign(rec_block, row_order):
    rows = lax.axis_size("row")
    size, rank = rec_block.shape
    wraps = (lax.axis_index("col") == lax.axis_size("col") - 1).astype(jnp.int32)
    index = (row_order + (rows - wraps)) % rows
    pieces = lax.all_to_all(
        rec_block.reshape(rows, size // rows, rank), "row", 0, 0, tiled=True
    )
    pieces = lax.all_to_all(pick(pieces, index), "row", 0, 0, tiled=True)
    return pieces.reshape(size, rank)


def later(array, before):
    return lax.optimization_barrier((array, before))[0]


def local(acquired_tiles, row_live, col_live, row_order, source_init, receiver_init):
    strata = acquired_tiles.shape[0]
    part = receiver_init.shape[0] // CHUNKS
    src, recs = source_init, [receiver_init]
    for stratum in range(strata):
        ahead = stratum + 1 < strata and stratum != 1
        tile = (acquired_tiles if stratum == 0 else later(acquired_tiles, src))[stratum]
        src, recs = step(stratum, len(recs), src, recs, tile, row_live, col_live)
        src, recs = step(
            stratum, CHUNKS if ahead else 1, src, recs, tile, row_live, col_live
        )
        if ahead:
            recs = [onward(rec, ("row", "col")) for rec in recs]
        elif stratum == 1:
            whole = reassign(recs[0], row_order)
            recs = [
                onward(whole[i * part : (i + 1) * part], "col") for i in range(CHUNKS)
            ]
    return src, recs[0]


def solution(mesh):
    placed = (
        P(None, ("row", "col"), None),
        P(None, ("row", "col")),
        P(None, ("row", "col")),
        P(),
        P(("row", "col"), None),
        P(("row", "col"), None),
    )
    return jax.shard_map(
        local,
        mesh=mesh,
        in_specs=placed,
        out_specs=(P(("row", "col"), None), P(("row", "col"), None)),
        check_vma=False,
    )
```

time: 161 us -> 172 us (1.068); the launches traced: 158 us -> 172 us
  Pallas kernels: 0 us -> 53.6 us
  waiting for transfers between devices: 103 us -> 65.3 us
  blocking collectives: 0 us -> 31.9 us
  matrix products: 29.1 us -> 0 us
  other arithmetic: 5.4 us -> 0.52 us
    pallas_call x0 -> x14, Pallas kernels: none -> 53.6 us  [the longest x1 33.7 us: pick(): pl.pallas_call(pick_body, out_shape=jax.ShapeDtypeStruct(pieces.shape, pi...]
    all_to_all x0 -> x1, blocking collectives: none -> 31.9 us  [reassign(): pieces = lax.all_to_all(pick(pieces, index), 'row', 0, 0, tiled=True)]
    dot_general x24 -> x0, matrix products: 29.1 us -> none  [the longest x8 11.8 us: fit_dense(): lax.dot_general(src_half, rec_half, (((1,), (1,)), ((), ())), preferred_e...]
    ppermute x3 -> x6, waiting for transfers between devices: 64.3 us -> 40.1 us  [onward(): lax.ppermute(block, axes, [(i, (i + 1) % count) for i in range(count)])]
    all_to_all x2 -> x1, waiting for transfers between devices: 38.5 us -> 25.1 us  [reassign(): lax.all_to_all(rec_block.reshape(rows, size // rows, rank), 'row', 0, 0,...]
    squeeze x0 -> x4, local copies, waits for them, and re-layouts: none -> 7.19 us  [local(): (acquired_tiles if stratum == 0 else later(acquired_tiles, src))[stratum]]
    ppermute x3 -> x6, starting transfers between devices: 0.25 us -> 5.54 us  [onward(): lax.ppermute(block, axes, [(i, (i + 1) % count) for i in range(count)])]
    all_to_all x2 -> x1, starting transfers between devices: 10.4 us -> 5.94 us  [reassign(): lax.all_to_all(rec_block.reshape(rows, size // rows, rank), 'row', 0, 0,...]
  transfers between devices with their start and end apart: 5 -> 7, of which waited for: 5 -> 7; matrix products, arithmetic and copies ran while one was open for 3% -> 3% of each run, Pallas kernels for 0% -> 3%
where the time goes in v1:
time: 172 us
  waiting for transfers between devices  65.3 us (38%)
  Pallas kernels  53.6 us (31%)
  blocking collectives  31.9 us (19%)
  starting transfers between devices  11.5 us (7%)
  local copies, waits for them, and re-layouts  8.49 us (5%)
    ppermute x6, waiting for transfers between devices, onward(): lax.ppermute(block, axes, [(i, (i + 1) % count) for i in range(count)])  40.1 us
    pallas_call x1, Pallas kernels, pick(): pl.pallas_call(pick_body, out_shape=jax.ShapeDtypeStruct(pieces.shape, pi...  33.7 us
    all_to_all x1, blocking collectives, reassign(): pieces = lax.all_to_all(pick(pieces, index), 'row', 0, 0, tiled=True)  31.9 us
    all_to_all x1, waiting for transfers between devices, reassign(): lax.all_to_all(rec_block.reshape(rows, size // rows, rank), 'row', 0, 0,...  25.1 us
    pallas_call x13, Pallas kernels, step_part(): pl.pallas_call(functools.partial(step_body, stratum, part, width, parts,...  19.9 us
    squeeze x4, local copies, waits for them, and re-layouts, local(): (acquired_tiles if stratum == 0 else later(acquired_tiles, src))[stratum]  7.19 us
    all_to_all x1, starting transfers between devices, reassign(): lax.all_to_all(rec_block.reshape(rows, size // rows, rank), 'row', 0, 0,...  5.94 us
    ppermute x6, starting transfers between devices, onward(): lax.ppermute(block, axes, [(i, (i + 1) % count) for i in range(count)])  5.54 us
  transfers between devices with their start and end apart: 7, of which 7 were waited for; matrix products, arithmetic and copies ran while one was open for 3% of the time, Pallas kernels for 3%

profile of v1, /device:TPU:0, one launch (start us, length us, event | category | flops | bytes accessed | tf_op | source)
XLA Modules:
  0.0 172.1 jit_solution(13414891215351394314)
XLA Ops:
  0.7 1.9 %slice_bitcast_fusion.3.refs_1_ = bf16[1024,1024]{1,0:T(8,128)(2,1)S(1)} fusion(bf16[4,1024,1024]{2,1,0:T(8,128)(2,1)} %param.6), kind=kLoop, calls=%fused_computation.3 | loop fusion | bytes 4194304 | tf_op jit(solution)/shard_map/squeeze | solution.py:145
  2.6 0.2 copy-done.3
  2.8 2.0 %shard_map.77 = (f32[1024,256]{1,0:T(8,128)S(1)}, f32[1024,256]{1,0:T(8,128)S(1)}) custom-call(f32[1024,256]{1,0:T(8,128)S(1)} %copy-done.2, bf16[1024,1024]{1,0:T(8,128)(2,1)S(1)} %slice_bitcast_fusion.3.refs_1_, s32[4,1024]{1,0:T(4,128)S(1)} %copy-done, s32[4,1024]{1,0:T(4,128)S(1)} %copy-done.1, f32[1024,256]{1,0:T(8,128)S(1)} %copy-done.3), custom_call_target="tpu_custom_call" | custom-call | flops 1610612736 | bytes 5242880 | tf_op jit(solution)/shard_map/pallas_call | solution.py:63
  4.8 1.2 shard_map.78
  6.0 1.2 shard_map.79
  7.3 1.8 %slice_bitcast_fusion.2.refs_1_ = bf16[1024,1024]{1,0:T(8,128)(2,1)S(1)} fusion(bf16[4,1024,1024]{2,1,0:T(8,128)(2,1)} %param.6), kind=kLoop, calls=%fused_computation.2 | loop fusion | bytes 4194304 | tf_op jit(solution)/shard_map/squeeze | solution.py:145
  9.1 12.0 %collective-permute-done.1.refs_4_ = f32[512,256]{1,0:T(8,128)S(1)} collective-permute-done((f32[512,256]{1,0:T(8,128)S(1)}, f32[512,256]{1,0:T(8,128)S(1)}, u32[]{:S(2)}, u32[]{:S(2)}) %collective-permute-start.1) | collective-permute-done | bytes 524320 | tf_op jit(solution)/shard_map/ppermute | solution.py:120
  21.1 1.2 shard_map.80
  22.3 4.4 %collective-permute-done.refs_4_ = f32[512,256]{1,0:T(8,128)S(1)} collective-permute-done((f32[512,256]{1,0:T(8,128)S(1)}, f32[512,256]{1,0:T(8,128)S(1)}, u32[]{:S(2)}, u32[]{:S(2)}) %collective-permute-start) | collective-permute-done | bytes 524320 | tf_op jit(solution)/shard_map/ppermute | solution.py:120
  26.7 1.2 shard_map.81
  27.9 2.9 %shard_map.82 = (f32[1024,256]{1,0:T(8,128)S(1)}, f32[1024,256]{1,0:T(8,128)}) custom-call(f32[1024,256]{1,0:T(8,128)S(1)} %get-tuple-element.37.refs_0_, bf16[1024,1024]{1,0:T(8,128)(2,1)S(1)} %slice_bitcast_fusion.2.refs_1_, s32[4,1024]{1,0:T(4,128)S(1)} %copy-done, s32[4,1024]{1,0:T(4,128)S(1)} %copy-done.1, f32[512,256]{1,0:T(8,128)S(1)} %get-tuple-element.38.refs_4_, ...), custom_call_target="tpu_custom_call" | custom-call | flops 1610612736 | bytes 5242880 | tf_op jit(solution)/shard_map/pallas_call | solution.py:63
  30.8 5.9 %all-to-all-start = ((f32[16,64,256]{2,1,0:T(8,128)}), f32[16,64,256]{2,1,0:T(8,128)S(1)}, u32[]{:S(2)}, u32[]{:S(2)}) async-start(f32[16,64,256]{2,1,0:T(8,128)} %bitcast.3), calls=%async_computation | async-start | bytes 2097152 | tf_op jit(solution)/shard_map/all_to_all | solution.py:128
  36.8 0.5 and_select_fusion.index_ref
  37.3 25.1 %all-to-all-done.pieces_ref = f32[16,64,256]{2,1,0:T(8,128)S(1)} async-done(((f32[16,64,256]{2,1,0:T(8,128)}), f32[16,64,256]{2,1,0:T(8,128)S(1)}, u32[]{:S(2)}, u32[]{:S(2)}) %all-to-all-start) | async-done | bytes 1048608 | tf_op jit(solution)/shard_map/all_to_all | solution.py:128
  62.4 1.0 copy-done.4
  63.4 33.7 %shard_map.83 = f32[16,64,256]{2,1,0:T(8,128)} custom-call(s32[16]{0:T(128)} %and_select_fusion.index_ref, f32[16,64,256]{2,1,0:T(8,128)} %copy-done.4), custom_call_target="tpu_custom_call" | custom-call | bytes 2097152 | tf_op jit(solution)/shard_map/pallas_call | solution.py:103
  97.1 31.9 %all_to_all.10 = f32[16,64,256]{2,1,0:T(8,128)S(1)} all-to-all(f32[16,64,256]{2,1,0:T(8,128)} %shard_map.83), channel_id=1, replica_groups=mesh['row'=16,'col'=16] {'row'}, dimensions={0} | all-to-all | bytes 2097152 | tf_op jit(solution)/shard_map/all_to_all | solution.py:131
  129.2 3.6 %collective-permute-start.2 = (f32[512,256]{1,0:T(8,128)S(1)}, f32[512,256]{1,0:T(8,128)S(1)}, u32[]{:S(2)}, u32[]{:S(2)}) collective-permute-start(f32[512,256]{1,0:T(8,128)S(1)} %bitcast.11), channel_id=1, source_target_pairs={{0,1},{1,2},{2,3},{3,4},{4,5},{5,6},{6,7},{7,8},{8,9},{9,10},{10,1... | collective-permute-start | bytes 1572872 | tf_op jit(solution)/shard_map/ppermute | solution.py:120
  132.8 1.8 %slice_bitcast_fusion.1.refs_1_ = bf16[1024,1024]{1,0:T(8,128)(2,1)S(1)} fusion(bf16[4,1024,1024]{2,1,0:T(8,128)(2,1)} %param.6), kind=kLoop, calls=%fused_computation.1 | loop fusion | bytes 4194304 | tf_op jit(solution)/shard_map/squeeze | solution.py:145
  134.6 5.3 %collective-permute-done.3.refs_4_ = f32[512,256]{1,0:T(8,128)S(1)} collective-permute-done((f32[512,256]{1,0:T(8,128)S(1)}, f32[512,256]{1,0:T(8,128)S(1)}, u32[]{:S(2)}, u32[]{:S(2)}) %collective-permute-start.3) | collective-permute-done | bytes 524320 | tf_op jit(solution)/shard_map/ppermute | solution.py:120
  139.9 1.2 shard_map.84
  141.1 4.4 %collective-permute-done.2.refs_4_ = f32[512,256]{1,0:T(8,128)S(1)} collective-permute-done((f32[512,256]{1,0:T(8,128)S(1)}, f32[512,256]{1,0:T(8,128)S(1)}, u32[]{:S(2)}, u32[]{:S(2)}) %collective-permute-start.2) | collective-permute-done | bytes 524320 | tf_op jit(solution)/shard_map/ppermute | solution.py:120
  145.5 1.2 shard_map.85
  146.7 1.2 shard_map.86
  148.0 1.2 shard_map.87
  149.2 1.6 collective-permute-start.4
  150.7 1.8 %slice_bitcast_fusion.refs_1_ = bf16[1024,1024]{1,0:T(8,128)(2,1)S(1)} fusion(bf16[4,1024,1024]{2,1,0:T(8,128)(2,1)} %param.6), kind=kLoop, calls=%fused_computation | loop fusion | bytes 4194304 | tf_op jit(solution)/shard_map/squeeze | solution.py:145
  152.5 9.5 %collective-permute-done.5.refs_4_ = f32[512,256]{1,0:T(8,128)S(1)} collective-permute-done((f32[512,256]{1,0:T(8,128)S(1)}, f32[512,256]{1,0:T(8,128)S(1)}, u32[]{:S(2)}, u32[]{:S(2)}) %collective-permute-start.5) | collective-permute-done | bytes 524320 | tf_op jit(solution)/shard_map/ppermute | solution.py:120
  162.0 1.2 shard_map.88
  163.1 4.5 %collective-permute-done.4.refs_4_ = f32[512,256]{1,0:T(8,128)S(1)} collective-permute-done((f32[512,256]{1,0:T(8,128)S(1)}, f32[512,256]{1,0:T(8,128)S(1)}, u32[]{:S(2)}, u32[]{:S(2)}) %collective-permute-start.4) | collective-permute-done | bytes 524320 | tf_op jit(solution)/shard_map/ppermute | solution.py:120
  167.6 1.2 shard_map.89
  168.8 3.3 %shard_map.90 = (f32[1024,256]{1,0:T(8,128)}, f32[1024,256]{1,0:T(8,128)}) custom-call(f32[1024,256]{1,0:T(8,128)S(1)} %get-tuple-element.53.refs_0_, bf16[1024,1024]{1,0:T(8,128)(2,1)S(1)} %slice_bitcast_fusion.refs_1_, s32[4,1024]{1,0:T(4,128)S(1)} %copy-done, s32[4,1024]{1,0:T(4,128)S(1)} %copy-done.1, f32[512,256]{1,0:T(8,128)S(1)} %get-tuple-element.54.refs_4_, ...), custom_call_target="tpu_custom_call" | custom-call | flops 1610612736 | bytes 5242880 | tf_op jit(solution)/shard_map/pallas_call | solution.py:63
  (15 shorter events, 0.4 us)
Async XLA Ops:
  0.6 2.0 %copy-start.2 = (f32[1024,256]{1,0:T(8,128)S(1)}, f32[1024,256]{1,0:T(8,128)}, u32[]{:S(2)}) copy-start(f32[1024,256]{1,0:T(8,128)} %refs_0_.1) | copy-start | bytes 3145732
  0.6 2.2 %copy-start.3 = (f32[1024,256]{1,0:T(8,128)S(1)}, f32[1024,256]{1,0:T(8,128)}, u32[]{:S(2)}) copy-start(f32[1024,256]{1,0:T(8,128)} %refs_4_.1) | copy-start | bytes 3145732
  0.7 2.2 %copy-start = (s32[4,1024]{1,0:T(4,128)S(1)}, s32[4,1024]{1,0:T(4,128)}, u32[]{:S(2)}) copy-start(s32[4,1024]{1,0:T(4,128)} %refs_2_.25) | copy-start | bytes 49156
  0.7 2.1 %copy-start.1 = (s32[4,1024]{1,0:T(4,128)S(1)}, s32[4,1024]{1,0:T(4,128)}, u32[]{:S(2)}) copy-start(s32[4,1024]{1,0:T(4,128)} %refs_3_.25) | copy-start | bytes 49156
  5.9 15.2 %collective-permute-start.1 = (f32[512,256]{1,0:T(8,128)S(1)}, f32[512,256]{1,0:T(8,128)S(1)}, u32[]{:S(2)}, u32[]{:S(2)}) collective-permute-start(f32[512,256]{1,0:T(8,128)S(1)} %get-tuple-element.35), channel_id=1, source_target_pairs={{0,1},{1,2},{2,3},{3,4},{4,5},{5,6},{6,7},{7,8},{8,9},{9,10},{10,1... | collective-permute-start | bytes 1572872 | tf_op jit(solution)/shard_map/ppermute | solution.py:120
  7.2 19.5 %collective-permute-start = (f32[512,256]{1,0:T(8,128)S(1)}, f32[512,256]{1,0:T(8,128)S(1)}, u32[]{:S(2)}, u32[]{:S(2)}) collective-permute-start(f32[512,256]{1,0:T(8,128)S(1)} %get-tuple-element.34), channel_id=1, source_target_pairs={{0,1},{1,2},{2,3},{3,4},{4,5},{5,6},{6,7},{7,8},{8,9},{9,10},{10,1... | collective-permute-start | bytes 1572872 | tf_op jit(solution)/shard_map/ppermute | solution.py:120
  30.8 6.0 %copy-start.5 = (s32[16]{0:T(128)S(1)}, s32[16]{0:T(128)}, u32[]{:S(2)}) copy-start(s32[16]{0:T(128)} %param.9) | copy-start | bytes 196
  30.8 31.6 %all-to-all-start = ((f32[16,64,256]{2,1,0:T(8,128)}), f32[16,64,256]{2,1,0:T(8,128)S(1)}, u32[]{:S(2)}, u32[]{:S(2)}) async-start(f32[16,64,256]{2,1,0:T(8,128)} %bitcast.3), calls=%async_computation | async-start | bytes 2097152 | tf_op jit(solution)/shard_map/all_to_all | solution.py:128
  62.4 1.0 copy-start.4
  129.1 10.8 %collective-permute-start.3 = (f32[512,256]{1,0:T(8,128)S(1)}, f32[512,256]{1,0:T(8,128)S(1)}, u32[]{:S(2)}, u32[]{:S(2)}) collective-permute-start(f32[512,256]{1,0:T(8,128)S(1)} %bitcast.12), channel_id=1, source_target_pairs={{0,1},{1,2},{2,3},{3,4},{4,5},{5,6},{6,7},{7,8},{8,9},{9,10},{10,1... | collective-permute-start | bytes 1572872 | tf_op jit(solution)/shard_map/ppermute | solution.py:120
  129.2 16.3 %collective-permute-start.2 = (f32[512,256]{1,0:T(8,128)S(1)}, f32[512,256]{1,0:T(8,128)S(1)}, u32[]{:S(2)}, u32[]{:S(2)}) collective-permute-start(f32[512,256]{1,0:T(8,128)S(1)} %bitcast.11), channel_id=1, source_target_pairs={{0,1},{1,2},{2,3},{3,4},{4,5},{5,6},{6,7},{7,8},{8,9},{9,10},{10,1... | collective-permute-start | bytes 1572872 | tf_op jit(solution)/shard_map/ppermute | solution.py:120
  147.9 14.1 %collective-permute-start.5 = (f32[512,256]{1,0:T(8,128)S(1)}, f32[512,256]{1,0:T(8,128)S(1)}, u32[]{:S(2)}, u32[]{:S(2)}) collective-permute-start(f32[512,256]{1,0:T(8,128)S(1)} %get-tuple-element.51), channel_id=1, source_target_pairs={{0,1},{1,2},{2,3},{3,4},{4,5},{5,6},{6,7},{7,8},{8,9},{9,10},{10,1... | collective-permute-start | bytes 1572872 | tf_op jit(solution)/shard_map/ppermute | solution.py:120
  149.2 18.4 %collective-permute-start.4 = (f32[512,256]{1,0:T(8,128)S(1)}, f32[512,256]{1,0:T(8,128)S(1)}, u32[]{:S(2)}, u32[]{:S(2)}) collective-permute-start(f32[512,256]{1,0:T(8,128)S(1)} %get-tuple-element.50), channel_id=1, source_target_pairs={{0,1},{1,2},{2,3},{3,4},{4,5},{5,6},{6,7},{7,8},{8,9},{9,10},{10,1... | collective-permute-start | bytes 1572872 | tf_op jit(solution)/shard_map/ppermute | solution.py:120
